TPU v7x, 128 devices: a whole 4x4x4 slice. The times are simulated.
128 devices in a mesh: dp: 16 (over x, y), seq: 8 (over z, core).
Axes of the slice: x: 4, y: 4, z: 4, core: 2. Of those that a mesh axis runs over, the one named last changes fastest.
Arguments:
- img_qkv: bfloat16 [16, 1024, 7680], P('dp', 'seq'), may hold values from -20 to 20
- text_cache: bfloat16 [128, 333, 2432], P('dp', None, 'seq'), may hold values from -6 to 6
- null_rows: bfloat16 [333, 2432], P(None, 'seq'), may hold values from -6 to 6
- w_text: bfloat16 [2432, 7680], P(None, 'seq'), may hold values from -0.125 to 0.125
- cache_owner: int32 [16], replicated, may hold values from 0 to 15, as said below
- cache_row: int32 [16], replicated, may hold values from 0 to 7
- dropped: int32 [16, 2], replicated, may hold values from 0 to 1, as said below
- text_length: int32 [16], replicated, may hold values from 78 to 333, as said below
- d_img_out: bfloat16 [16, 1024, 2560], P('dp', 'seq'), may hold values from -6 to 6
- d_text_out: bfloat16 [16, 333, 2560], P('dp', None, 'seq'), may hold values from -6 to 6
Outputs:
- img_out: bfloat16 [16, 1024, 2560], P('dp', 'seq')
- text_out: bfloat16 [16, 333, 2560], P('dp', None, 'seq')
- d_img_qkv: bfloat16 [16, 1024, 7680], P('dp', 'seq')
- d_w_text: float32 [2432, 7680], P('dp', 'seq')
Inputs may be any that keep to these rules, and one draw needn't show every extreme that they name: cache_owner is a permutation: every index of dp owns the caption of exactly one sample. No sample has both parts dropped. `text_length`: some sample has the length 333.
All inputs are finite; a program needn't handle non-finite values.
Results may differ from a plain program's by a relative error of at most 0.012.
The roundings to bfloat16 on the way count: a program that leaves them out, or rounds other values in their place, can miss the bound.
Values may be sent and summed in bfloat16 or wider, within the bound.
A program may use at most 128 MiB of HBM per device.

v0:
```python
import functools

import jax
import jax.numpy as jnp
from jax import lax
from jax.experimental import pallas as pl
from jax.experimental.pallas import tpu as pltpu
from jax.sharding import PartitionSpec as P

HD = 64
CLIP = 77
BQ = 256
KC = 464
f32, bf16 = jnp.float32, jnp.bfloat16


def chunks(n, c):
    return [(s, min(c, n - s)) for s in range(0, n, c)]


def dot(a, b):
    return jnp.dot(a, b, preferred_element_type=f32)


def fold(x, op):
    parts = [x[8 * i : 8 * i + 8] for i in range(x.shape[0] // 8)]
    while len(parts) > 1:
        parts = [
            op(parts[j], parts[j + 1]) if j + 1 < len(parts) else parts[j]
            for j in range(0, len(parts), 2)
        ]
    return parts[0]


def forward_block(i, img, nk, x, xt, bias, s_scr, e_scr, state, wq=BQ):
    w_probs, w_values, w_keys, delta, attended = state
    q0 = pl.multiple_of(i * BQ, BQ)
    zeros = jnp.zeros((HD, wq), bf16)
    q_t = xt[0:64, pl.ds(q0, wq)] * bf16(0.125)
    w_scores = jnp.concatenate([zeros, q_t], 0)
    top8 = None
    for k, n in chunks(nk, KC):
        s = dot(x[k : k + n, 0:128], w_scores)
        if k + n > img:
            b = bias[max(k - img, 0) : k + n - img, :]
            b = jnp.concatenate([b] * (wq // 128), 1)
            s = s + b if k >= img else jnp.concatenate([s[: img - k], s[img - k :] + b], 0)
        s_scr[k : k + n, 0:wq] = s
        c = fold(s, jnp.maximum)
        top8 = c if top8 is None else jnp.maximum(top8, c)
        yield
    top = jnp.max(top8, 0, keepdims=True)
    sum8 = out_t = None
    for k, n in chunks(nk, KC):
        e = jnp.exp(s_scr[k : k + n, 0:wq] - top)
        c = fold(e, jnp.add)
        sum8 = c if sum8 is None else sum8 + c
        e = e.astype(bf16)
        e_scr[k : k + n, 0:wq] = e
        o = dot(xt[128:192, k : k + n], e)
        out_t = o if out_t is None else out_t + o
        yield
    cot_t = xt[192:256, pl.ds(q0, wq)].astype(f32)
    inv = 1.0 / jnp.sum(sum8, 0, keepdims=True)
    out_t = (out_t * inv).astype(bf16)
    row_delta = jnp.sum(cot_t * out_t.astype(f32), 0, keepdims=True) * inv
    cot_s = (cot_t * inv).astype(bf16)
    w_probs[:, 0:wq] = jnp.concatenate([cot_s, zeros], 0)
    w_values[0:wq, :] = jnp.concatenate([zeros, cot_s], 0).T
    w_keys[0:wq, :] = jnp.concatenate([q_t, zeros], 0).T
    delta[:, 0:wq] = jnp.broadcast_to(row_delta, (delta.shape[0], wq))
    attended[:, 0:wq] = out_t


def backward_block(i, nk, x, xt, e_scr, state, acc, out, attended_t, wq=BQ):
    w_probs, w_values, w_keys, delta, attended = state
    q0 = pl.multiple_of(i * BQ, BQ)
    row_delta = delta[0:1, 0:wq]
    dq_t = None
    for k, n in chunks(nk, KC):
        dp = dot(x[k : k + n, 128:256], w_probs[:, 0:wq])
        e = e_scr[k : k + n, 0:wq]
        ds = (e.astype(f32) * (dp - row_delta)).astype(bf16)
        d = dot(xt[64:128, k : k + n], ds)
        dq_t = d if dq_t is None else dq_t + d
        acc[k : k + n, :] += dot(ds, w_keys[0:wq, :]) + dot(e, w_values[0:wq, :])
        yield
    dq_t = (dq_t * 0.125).astype(bf16)
    out[pl.ds(q0, wq), 0:128] = jnp.concatenate([dq_t, attended[:, 0:wq]], 0).T
    attended_t[:, pl.ds(q0, wq)] = attended[:, 0:wq]


def alternate(a, b):
    live = [True, True]
    turn = 0
    while live[0] or live[1]:
        g = 1 if turn % 3 == 2 else 0
        turn += 1
        if live[g]:
            live[g] = next((a, b)[g], "end") is None


def all_blocks(n, img, nk, x, xt, bias, s_scr, e_scrs, states, acc, out, attended_t):
    last = -(-(nk - (n - 1) * BQ) // 128) * 128

    def forward(i, side, wq=BQ):
        return forward_block(i, img, nk, x, xt, bias, s_scr, e_scrs[side], states[side], wq)

    def backward(i, side, wq=BQ):
        return backward_block(
            i, nk, x, xt, e_scrs[side], states[side], acc, out, attended_t, wq
        )

    for _ in forward(0, 0):
        pass

    def body(j, c):
        alternate(forward(2 * j + 1, 1), backward(2 * j, 0))
        alternate(forward(2 * j + 2, 0), backward(2 * j + 1, 1))
        return c

    lax.fori_loop(0, n // 2 - 1, body, 0)
    alternate(forward(n - 1, 1, last), backward(n - 2, 0))
    for _ in backward(n - 1, 1, last):
        pass


def swap_halves(v):
    return jnp.concatenate([v[:, HD:], v[:, :HD]], 1)


def low_lanes(shape):
    return lax.broadcasted_iota(jnp.int32, shape, 1) < HD


def split_pair(t0, t1, t2, cot):
    low = low_lanes(t0.shape)
    r1, r2, rc = swap_halves(t1), swap_halves(t2), swap_halves(cot)
    return (t0, jnp.where(low, t1, rc)), (jnp.where(low, r1, r2), jnp.where(low, r2, cot))


def join_pair(a0, b0, a1, b1):
    low = low_lanes(a0.shape)
    ra0, rb0, ra1 = swap_halves(a0), swap_halves(b0), swap_halves(a1)
    return (
        jnp.where(low, a0, rb0),
        jnp.where(low, rb0, ra1),
        b1,
        jnp.where(low, ra0, a1),
    )


def tiles_of(rows, lanes):
    return [(r, c) for r in range(0, rows, 16) for c in range(0, lanes, 128)]


GROUPS = (
    ((0, 128), None),
    ((128, 256), (256, 384)),
    (None, (384, 512)),
    ((512, 640), (640, 768)),
    ((768, 896), (896, 1024)),
)


def kernel(
    dims,
    qkv,
    cot_img,
    cache,
    null_rows,
    w_hbm,
    owner,
    cache_row,
    dropped,
    length,
    cot_text,
    back,
    text_out,
    d_w,
    packed,
    x_all,
    out_all,
    attended_t,
    w_t,
    rows_t,
    text_qkv,
    text_cot,
    raw,
    null_pad,
    pieces,
    pieces_in,
    pieces_out,
    pieces_got,
    d_text,
    term,
    term_in,
    part,
    part_in,
    bias,
    xt,
    s_scr,
    e_scr0,
    e_scr1,
    acc,
    st_a0,
    st_a1,
    st_b0,
    st_b1,
    st_c0,
    st_c1,
    st_d0,
    st_d1,
    st_e0,
    st_e1,
    sem_w,
    sems_a,
    sems_b,
    sems_c,
    sems_f,
    sems_in,
    sems_out,
    sems_1,
    sems_2,
):
    n_dp, n_seq, nx, ny = dims
    dp, me = lax.axis_index("dp"), lax.axis_index("seq")
    mx, my = dp // ny, dp % ny
    tokens = qkv.shape[0]
    heads = x_all.shape[0]
    nq = xt.shape[1]
    n_x = x_all.shape[1]
    img = tokens * n_seq
    nk = e_scr0.shape[0]
    e_scrs = (e_scr0, e_scr1)
    states = ((st_a0, st_b0, st_c0, st_d0, st_e0), (st_a1, st_b1, st_c1, st_d1, st_e1))
    txt_pad = nk - img
    depth, txt = null_rows.shape
    lanes = raw.shape[1]
    per = pieces.shape[1]
    chunk_rows = d_w.shape[0]

    def remote(src, dst, sems, at, dev):
        return pltpu.make_async_remote_copy(
            src_ref=src,
            dst_ref=dst,
            send_sem=sems.at[(0,) + at],
            recv_sem=sems.at[(1,) + at],
            device_id=dev,
            device_id_type=pl.DeviceIdType.MESH,
        )

    def each(n, fn, start=0):
        def body(i, c):
            fn(i)
            return c

        lax.fori_loop(start, n, body, 0)

    barrier = pltpu.get_barrier_semaphore()

    def greet_seq(o):
        pl.semaphore_signal(
            barrier, inc=1, device_id=(dp, me ^ o), device_id_type=pl.DeviceIdType.MESH
        )

    def greet_dp(o):
        pl.semaphore_signal(
            barrier, inc=1, device_id=(dp ^ o, me), device_id_type=pl.DeviceIdType.MESH
        )

    each(n_seq, greet_seq, 1)
    each(n_dp, greet_dp, 1)
    w_copy = pltpu.make_async_copy(w_hbm, w_t, sem_w)
    w_copy.start()

    mine = jnp.int32(0)
    for b in range(n_dp):
        mine = jnp.where(owner[b] == dp, jnp.int32(b), mine)
    row = cache_row[mine]
    raw[...] = jnp.zeros_like(raw)
    raw[:, 0:txt] = cache[row]
    null_pad[...] = jnp.zeros_like(null_pad)
    null_pad[:, 0:txt] = null_rows[...]
    tiles = tiles_of(depth, lanes)
    for t, (r, c) in enumerate(tiles):
        pieces[t // per, t % per] = raw[r : r + 16, c : c + 128]
    for t in range(len(tiles), n_dp * per):
        pieces[t // per, t % per] = jnp.zeros((16, 128), bf16)
    pieces_in[dp] = pieces[dp]

    def pack(p):
        c = pl.multiple_of(p * 384, 128)
        t = [qkv[:, pl.ds(pl.multiple_of(c + 128 * j, 128), 128)] for j in range(3)]
        g = cot_img[:, pl.ds(pl.multiple_of(p * 128, 128), 128)]
        for j, (a, b) in enumerate(split_pair(*t, g)):
            head = 2 * p + j
            to, h = head // heads, head % heads
            packed[to, h, :, 0:128] = a
            packed[to, h, :, 128:256] = b

    lax.fori_loop(0, n_seq, lambda i, c: (pack(i * heads // 2), c)[1], 0, unroll=2)

    pl.semaphore_wait(barrier, n_seq + n_dp - 2)

    def send_a(o):
        return remote(pieces.at[dp ^ o], pieces_in.at[dp], sems_a, (o,), (dp ^ o, me))

    def recv_a(o):
        return remote(pieces.at[dp], pieces_in.at[dp ^ o], sems_a, (o,), (dp ^ o, me))

    each(n_dp, lambda o: send_a(o).start(), 1)

    mine_rows = pl.ds(pl.multiple_of(me * tokens, tokens), tokens)

    def peer_rows(o):
        return pl.ds(pl.multiple_of((me ^ o) * tokens, tokens), tokens)

    def send_in(h, o):
        return remote(
            packed.at[me ^ o, h], x_all.at[h, mine_rows], sems_in, (h, o), (dp, me ^ o)
        )

    def recv_in(h, o):
        return remote(
            packed.at[me, h], x_all.at[h, peer_rows(o)], sems_in, (h, o), (dp, me ^ o)
        )

    each(n_seq, lambda o: send_in(0, o).start(), 1)

    each(n_dp, lambda o: recv_a(o).wait_recv(), 1)
    for b in range(n_dp):
        pieces_out[b] = pieces_in[owner[b]]

    def send_b(o):
        return remote(pieces_out.at[dp ^ o], pieces_got.at[dp], sems_b, (o,), (dp ^ o, me))

    def recv_b(o):
        return remote(pieces_out.at[dp], pieces_got.at[dp ^ o], sems_b, (o,), (dp ^ o, me))

    each(n_dp, lambda o: send_b(o).start(), 1)
    pieces_got[dp] = pieces_out[dp]

    text_cot[...] = jnp.zeros_like(text_cot)
    text_cot[:, 0:txt] = cot_text[...]
    if nq > n_x:
        xt[:, n_x:nq] = jnp.zeros((256, nq - n_x), bf16)
    seen = lax.broadcasted_iota(jnp.int32, bias.shape, 0) < length[dp]
    bias[...] = jnp.where(seen, 0.0, -1e30)
    drop_clip, drop_t5 = dropped[0, dp], dropped[1, dp]

    each(n_dp, lambda o: recv_b(o).wait_recv(), 1)
    for t, (r, c) in enumerate(tiles):
        got = pieces_got[t // per, t % per].astype(f32)
        token = lax.broadcasted_iota(jnp.int32, (16, 128), 1) + c
        drop = jnp.where(token < CLIP, drop_clip, drop_t5)
        own = null_pad[r : r + 16, c : c + 128].astype(f32)
        at = pl.ds(pl.multiple_of(me * depth + r, 16), 16)
        rows_t[at, c : c + 128] = jnp.where(drop == 1, own, got).astype(bf16)

    def block(s):
        return rows_t.at[pl.ds(pl.multiple_of(s * depth, 16), depth)]

    def send_c(o):
        return remote(block(me), block(me), sems_c, (o,), (dp, me ^ o))

    def recv_c(o):
        return remote(block(me), block(me ^ o), sems_c, (o,), (dp, me ^ o))

    def send_f(o):
        return remote(block(me ^ o), block(me ^ o), sems_f, (o,), (dp, me ^ 1))

    def recv_f(o):
        return remote(block(me ^ 1), block(me ^ 1 ^ o), sems_f, (o,), (dp, me ^ 1))

    far = sorted(range(2, n_seq, 2), key=lambda o: o == n_seq // 2)
    for o in far[::-1] + [1]:
        send_c(o).start()
    def pack_rest(i):
        for j in (1, 3, 4):
            pack(i * heads + j)

    each(n_seq // 2, pack_rest)
    for h in range(1, heads):
        each(n_seq, lambda o: send_in(h, o).start(), 1)

    def own_image(h):
        x_all[h, mine_rows, :] = packed[me, h]

    each(heads, own_image)
    for o in far:
        recv_c(o).wait_recv()
        send_f(o).start()
    recv_c(1).wait_recv()
    for o in far:
        recv_f(o).wait_recv()
    w_copy.wait()
    half = w_t.shape[0] // 2
    for r in range(0, w_t.shape[0], half):
        text_qkv[r : r + half, :] = dot(w_t[r : r + half, :], rows_t[...]).astype(bf16)

    def send_out(h, o):
        return remote(
            out_all.at[h, peer_rows(o)], back.at[h, me], sems_out, (h, o), (dp, me ^ o)
        )

    def recv_out(h, o):
        return remote(
            out_all.at[h, mine_rows], back.at[h, me ^ o], sems_out, (h, o), (dp, me ^ o)
        )

    def ranges(g, side):
        lo, hi = GROUPS[g][side]
        return pl.ds(lo, hi - lo)

    def along(side, o):
        return (mx * ny + (my ^ o), me) if side == 0 else ((mx ^ o) * ny + my, me)

    def first(g, side, o, sending):
        here = my if side == 0 else mx
        other = here ^ o
        to = other if sending else here
        lane = ranges(g, side)
        src = term.at[:, to, :, lane] if side == 0 else term.at[to, :, :, lane]
        slot = here if sending else other
        return remote(
            src, term_in.at[side, slot, :, :, lane], sems_1, (g, side, o), along(side, o)
        )

    def second(g, side, o, sending):
        here = mx if side == 0 else my
        other = here ^ o
        lane = ranges(g, side)
        to = other if sending else here
        slot = here if sending else other
        return remote(
            part.at[to, :, lane],
            part_in.at[slot, :, lane],
            sems_2,
            (g, side, o),
            along(1 - side, o),
        )

    def sides_of(g):
        return [side for side in range(2) if GROUPS[g][side] is not None]

    def finish_heads(g):
        sides = sides_of(g)
        lo, hi = GROUPS[g][sides[0]][0], GROUPS[g][sides[-1]][1]
        a1, b1 = [out_all[g, img:nk, c : c + 128] for c in (0, 128)]
        low = low_lanes(a1.shape)
        if g % 2:
            b0 = out_all[g - 1, img:nk, 128:256]
            d_text[:, lo : lo + 128] = jnp.where(low, swap_halves(b0), swap_halves(a1))
            d_text[:, lo + 128 : lo + 256] = b1
        else:
            rb = swap_halves(b1)
            d_text[:, lo : lo + 128] = jnp.where(low, a1, rb)
            if hi - lo > 128:
                d_text[:, lo + 128 : hi] = jnp.where(low, rb, jnp.zeros_like(rb))
        run = 4 * chunk_rows

        def multiply(x):
            a = rows_t[pl.ds(pl.multiple_of(x * run, 16), run), 0:txt_pad]
            d = dot(a, d_text[:, lo:hi])
            pad = jnp.zeros((term.shape[2] - chunk_rows, hi - lo), f32)
            for j in range(4):
                v = jnp.concatenate([d[j * chunk_rows : (j + 1) * chunk_rows], pad], 0)
                i = 4 * x + j
                term[i // ny, i % ny, :, lo:hi] = v.astype(bf16)

        each(nx * ny // 4, multiply)
        for side in sides_of(g):
            for o in range(1, ny if side == 0 else nx):
                first(g, side, o, True).start()

    def add_first(g):
        for side in sides_of(g):
            k = ny if side == 0 else nx
            for o in range(1, k):
                first(g, side, o, False).wait_recv()
            here = my if side == 0 else mx
            lane = ranges(g, side)

            def add(j):
                own = term[j, here, :, lane] if side == 0 else term[here, j, :, lane]
                total = own.astype(f32)
                for o in range(1, k):
                    total = total + term_in[side, here ^ o, j, :, lane].astype(f32)
                part[j, :, lane] = total.astype(bf16)

            n = nx if side == 0 else ny
            each(n, add)
            for o in range(1, n):
                second(g, side, o, True).start()

    def add_second(g):
        for side in sides_of(g):
            n = nx if side == 0 else ny
            for o in range(1, n):
                second(g, side, o, False).wait_recv()
            here = mx if side == 0 else my
            lane = ranges(g, side)
            total = part[here, :, lane].astype(f32)
            for o in range(1, n):
                total = total + part_in[here ^ o, :, lane].astype(f32)
            size = min(lane.start + lane.size, d_w.shape[1]) - lane.start
            d_w[:, lane.start : lane.start + size] = total[0:chunk_rows, 0:size]

    def one_head(h):
        wide = 3 * HD
        w_rows = pl.ds(pl.multiple_of(h * wide, HD), wide)
        xt[0:wide, img:n_x] = text_qkv[w_rows, :]
        head_rows = pl.ds(pl.multiple_of(h * HD, HD), HD)
        xt[wide:256, img:n_x] = text_cot[head_rows, :]
        x, out = x_all.at[h], out_all.at[h]
        x[img:n_x, :] = xt[:, img:n_x].T
        acc[...] = jnp.zeros_like(acc)
        each(n_seq, lambda o: recv_in(h, o).wait_recv(), 1)
        for r in range(0, img, BQ):
            xt[:, r : r + BQ] = x[r : r + BQ, :].T
        all_blocks(
            nq // BQ, img, nk, x, xt, bias, s_scr, e_scrs, states, acc, out, attended_t
        )
        for k, n in chunks(nk, KC):
            out[k : k + n, 128:256] = acc[k : k + n, :].astype(bf16)
        each(n_seq, lambda o: send_out(h, o).start(), 1)
        back[h, me] = out[mine_rows, :]
        text_out[head_rows, :] = attended_t[:, img : img + txt]
        for g in range(len(GROUPS)):
            pl.when(h == g)(functools.partial(finish_heads, g))
        for g in range(len(GROUPS)):
            if g + 2 < len(GROUPS):
                pl.when(h == g + 2)(functools.partial(add_second, g))
            if g + 1 < len(GROUPS):
                pl.when(h == g + 1)(functools.partial(add_first, g))

    each(heads, one_head)

    add_second(len(GROUPS) - 2)
    add_first(len(GROUPS) - 1)
    for h in range(heads):
        each(n_seq, lambda o: recv_out(h, o).wait_recv(), 1)
    add_second(len(GROUPS) - 1)

    each(n_dp, lambda o: send_a(o).wait_send(), 1)
    each(n_dp, lambda o: send_b(o).wait_send(), 1)
    for o in far + [1]:
        send_c(o).wait_send()
    for o in far:
        send_f(o).wait_send()
    for h in range(heads):
        each(n_seq, lambda o: send_in(h, o).wait_send(), 1)
        each(n_seq, lambda o: send_out(h, o).wait_send(), 1)
    for g in range(len(GROUPS)):
        for side in sides_of(g):
            for o in range(1, ny if side == 0 else nx):
                first(g, side, o, True).wait_send()
            for o in range(1, nx if side == 0 else ny):
                second(g, side, o, True).wait_send()


def unpack_kernel(back, text_in, d_w_in, img_out, text_out, d_qkv, d_w):
    heads, n_seq = back.shape[0], back.shape[1]
    for p in range(n_seq * heads // 2):
        v = []
        for j in range(2):
            s, h = divmod(2 * p + j, heads)
            v += [back[h, s, :, 0:128], back[h, s, :, 128:256]]
        t = join_pair(*v)
        for j in range(3):
            d_qkv[:, p * 384 + 128 * j : p * 384 + 128 * j + 128] = t[j]
        img_out[:, p * 128 : p * 128 + 128] = t[3]
    text_out[...] = text_in[...]
    d_w[...] = d_w_in[...]


def on_device(
    img_qkv,
    text_cache,
    null_rows,
    w_text,
    cache_owner,
    cache_row,
    dropped,
    text_length,
    d_img_out,
    d_text_out,
):
    n_dp, n_seq = lax.axis_size("dp"), lax.axis_size("seq")
    ny = 4
    nx = n_dp // ny
    txt, depth = null_rows.shape
    tokens = img_qkv.shape[1]
    width = w_text.shape[1]
    heads = width // (3 * HD)
    img = tokens * n_seq
    nk = -(-(img + txt) // 16) * 16
    nq = -(-(img + txt) // BQ) * BQ
    txt_pad = nk - img
    lanes = -(-txt // 128) * 128
    per = -(-(depth // 16 * (lanes // 128)) // n_dp)
    chunk_rows = depth * n_seq // n_dp
    chunk_pad = -(-chunk_rows // 16) * 16
    wide = -(-width // 128) * 128
    vmem = pl.BlockSpec(memory_space=pltpu.VMEM)
    smem = pl.BlockSpec(memory_space=pltpu.SMEM)
    dma = pltpu.SemaphoreType.DMA
    out_shape = (
        jax.ShapeDtypeStruct((heads, n_seq, tokens, 256), bf16),
        jax.ShapeDtypeStruct((heads * HD, txt), bf16),
        jax.ShapeDtypeStruct((chunk_rows, width), f32),
    )
    scratch = [
        pltpu.VMEM((n_seq, heads, tokens, 256), bf16),
        pltpu.VMEM((heads, img + lanes, 256), bf16),
        pltpu.VMEM((heads, nq, 256), bf16),
        pltpu.VMEM((HD, nq), bf16),
        pltpu.VMEM((width, n_seq * depth), bf16),
        pltpu.VMEM((n_seq * depth, lanes), bf16),
        pltpu.VMEM((width, lanes), bf16),
        pltpu.VMEM((heads * HD, lanes), bf16),
        pltpu.VMEM((depth, lanes), bf16),
        pltpu.VMEM((depth, lanes), bf16),
        pltpu.VMEM((n_dp, per, 16, 128), bf16),
        pltpu.VMEM((n_dp, per, 16, 128), bf16),
        pltpu.VMEM((n_dp, per, 16, 128), bf16),
        pltpu.VMEM((n_dp, per, 16, 128), bf16),
        pltpu.VMEM((txt_pad, wide), bf16),
        pltpu.VMEM((nx, ny, chunk_pad, wide), bf16),
        pltpu.VMEM((2, ny, nx, chunk_pad, wide), bf16),
        pltpu.VMEM((nx, chunk_pad, wide), bf16),
        pltpu.VMEM((nx, chunk_pad, wide), bf16),
        pltpu.VMEM((txt_pad, 128), f32),
        pltpu.VMEM((256, nq), bf16),
        pltpu.VMEM((nk, BQ), f32),
        pltpu.VMEM((nk, BQ), bf16),
        pltpu.VMEM((nk, BQ), bf16),
        pltpu.VMEM((nk, 128), f32),
        pltpu.VMEM((128, BQ), bf16),
        pltpu.VMEM((128, BQ), bf16),
        pltpu.VMEM((BQ, 128), bf16),
        pltpu.VMEM((BQ, 128), bf16),
        pltpu.VMEM((BQ, 128), bf16),
        pltpu.VMEM((BQ, 128), bf16),
        pltpu.VMEM((8, BQ), f32),
        pltpu.VMEM((8, BQ), f32),
        pltpu.VMEM((HD, BQ), bf16),
        pltpu.VMEM((HD, BQ), bf16),
        dma,
        dma((2, n_dp)),
        dma((2, n_dp)),
        dma((2, n_seq)),
        dma((2, n_seq)),
        dma((2, heads, n_seq)),
        dma((2, heads, n_seq)),
        dma((2, len(GROUPS), 2, max(nx, ny))),
        dma((2, len(GROUPS), 2, max(nx, ny))),
    ]
    back, text_out, d_w = pl.pallas_call(
        functools.partial(kernel, (n_dp, n_seq, nx, ny)),
        out_shape=out_shape,
        in_specs=[vmem, vmem, vmem, vmem, pl.BlockSpec(memory_space=pl.ANY)]
        + [smem] * 4
        + [vmem],
        out_specs=(vmem,) * 3,
        scratch_shapes=scratch,
        compiler_params=pltpu.CompilerParams(
            collective_id=0, has_side_effects=True, vmem_limit_bytes=62 * 2**20
        ),
    )(
        img_qkv[0],
        d_img_out[0],
        text_cache.transpose(0, 2, 1),
        null_rows.T,
        w_text.T,
        cache_owner,
        cache_row,
        dropped.T,
        text_length,
        d_text_out[0].T,
    )
    steps = 4
    part = tokens // steps
    whole = [pl.BlockSpec(a.shape, lambda i: (0, 0)) for a in (text_out, d_w)]
    img_out, text_out, d_qkv, d_w = pl.pallas_call(
        unpack_kernel,
        grid=(steps,),
        out_shape=(
            jax.ShapeDtypeStruct((tokens, n_seq * heads * HD), bf16),
            jax.ShapeDtypeStruct(text_out.shape, bf16),
            jax.ShapeDtypeStruct((tokens, n_seq * width), bf16),
            jax.ShapeDtypeStruct(d_w.shape, f32),
        ),
        in_specs=[pl.BlockSpec((heads, n_seq, part, 256), lambda i: (0, 0, i, 0))] + whole,
        out_specs=(
            pl.BlockSpec((part, n_seq * heads * HD), lambda i: (i, 0)),
            whole[0],
            pl.BlockSpec((part, n_seq * width), lambda i: (i, 0)),
            whole[1],
        ),
        compiler_params=pltpu.CompilerParams(vmem_limit_bytes=62 * 2**20),
    )(back, text_out, d_w)
    return (img_out[None], text_out.T[None], d_qkv[None], d_w)


def solution(mesh):
    return jax.shard_map(
        on_device,
        mesh=mesh,
        in_specs=(
            P("dp", "seq", None),
            P("dp", None, "seq"),
            P(None, "seq"),
            P(None, "seq"),
            P(),
            P(),
            P(),
            P(),
            P("dp", "seq", None),
            P("dp", None, "seq"),
        ),
        out_specs=(
            P("dp", "seq", None),
            P("dp", None, "seq"),
            P("dp", "seq", None),
            P("dp", "seq"),
        ),
        check_vma=False,
    )
```

profile of v0, /device:TPU:1, one launch (start us, length us, event | category | flops | bytes accessed | tf_op | source)
XLA Modules:
  0.0 118.3 jit_solution(3031408039239647802)
XLA Ops:
  0.6 112.8 %shard_map.129 = (bf16[5,8,128,256]{3,2,1,0:T(8,128)(2,1)}, bf16[320,333]{1,0:T(8,128)(2,1)}, f32[152,960]{1,0:T(8,128)}) custom-call(bf16[128,7680]{1,0:T(8,128)(2,1)} %bitcast.15, bf16[128,2560]{1,0:T(8,128)(2,1)} %bitcast.17, bf16[8,304,333]{2,1,0:T(8,128)(2,1)} %bitcast.16, bf16[304,333]{1,0:T(8,128)(2,1)} %bitcast.19, bf16[960,2432]{1,0:T(8,128)(2,1)} %bitcast.14, ...), custom_call_target="tpu_custom_call" | custom-call | tf_op jit(solution)/shard_map/pallas_call | solution.py:660
  113.4 4.9 %shard_map.130 = (bf16[128,2560]{1,0:T(8,128)(2,1)}, bf16[320,333]{1,0:T(8,128)(2,1)}, bf16[128,7680]{1,0:T(8,128)(2,1)}, f32[152,960]{1,0:T(8,128)}) custom-call(bf16[5,8,128,256]{3,2,1,0:T(8,128)(2,1)} %get-tuple-element.11.back, bf16[320,333]{1,0:T(8,128)(2,1)} %get-tuple-element.12.text_in, f32[152,960]{1,0:T(8,128)} %get-tuple-element.13.d_w_in), custom_call_target="tpu_custom_call" | custom-call | tf_op jit(solution)/shard_map/pallas_call | solution.py:686
where the time goes:
time: 118 us
  Pallas kernels  118 us (100%)
    pallas_call x1, Pallas kernels, on_device(): pl.pallas_call(functools.partial(kernel, (n_dp, n_seq, nx, ny)), out_shap...  113 us
    pallas_call x1, Pallas kernels, on_device(): pl.pallas_call(unpack_kernel, grid=(steps,), out_shape=(jax.ShapeDtypeStr...  4.87 us

commit v1 on v0

--- a/solution.py
+++ b/solution.py
@@ -680,7 +680,7 @@
         text_length,
         d_text_out[0].T,
     )
-    steps = 4
+    steps = 2
     part = tokens // steps
     whole = [pl.BlockSpec(a.shape, lambda i: (0, 0)) for a in (text_out, d_w)]
     img_out, text_out, d_qkv, d_w = pl.pallas_call(

time: 118 us -> 117 us (level)
  no operation moved by 1% of the time
where the time goes in v1:
time: 117 us
  Pallas kernels  117 us (100%)
    pallas_call x1, Pallas kernels, on_device(): pl.pallas_call(functools.partial(kernel, (n_dp, n_seq, nx, ny)), out_shap...  113 us
    pallas_call x1, Pallas kernels, on_device(): pl.pallas_call(unpack_kernel, grid=(steps,), out_shape=(jax.ShapeDtypeStr...  3.73 us

profile of v1, /device:TPU:1, one launch (start us, length us, event | category | flops | bytes accessed | tf_op | source)
XLA Modules:
  0.0 117.2 jit_solution(15550006037843689436)
XLA Ops:
  0.6 112.8 %shard_map.129 = (bf16[5,8,128,256]{3,2,1,0:T(8,128)(2,1)}, bf16[320,333]{1,0:T(8,128)(2,1)}, f32[152,960]{1,0:T(8,128)}) custom-call(bf16[128,7680]{1,0:T(8,128)(2,1)} %bitcast.15, bf16[128,2560]{1,0:T(8,128)(2,1)} %bitcast.17, bf16[8,304,333]{2,1,0:T(8,128)(2,1)} %bitcast.16, bf16[304,333]{1,0:T(8,128)(2,1)} %bitcast.19, bf16[960,2432]{1,0:T(8,128)(2,1)} %bitcast.14, ...), custom_call_target="tpu_custom_call" | custom-call | tf_op jit(solution)/shard_map/pallas_call | solution.py:660
  113.4 3.7 %shard_map.130 = (bf16[128,2560]{1,0:T(8,128)(2,1)}, bf16[320,333]{1,0:T(8,128)(2,1)}, bf16[128,7680]{1,0:T(8,128)(2,1)}, f32[152,960]{1,0:T(8,128)}) custom-call(bf16[5,8,128,256]{3,2,1,0:T(8,128)(2,1)} %get-tuple-element.11.back, bf16[320,333]{1,0:T(8,128)(2,1)} %get-tuple-element.12.text_in, f32[152,960]{1,0:T(8,128)} %get-tuple-element.13.d_w_in), custom_call_target="tpu_custom_call" | custom-call | tf_op jit(solution)/shard_map/pallas_call | solution.py:686

commit v2 on v1

--- a/solution.py
+++ b/solution.py
@@ -524,11 +524,11 @@
         )
         for k, n in chunks(nk, KC):
             out[k : k + n, 128:256] = acc[k : k + n, :].astype(bf16)
+        for g in range(len(GROUPS)):
+            pl.when(h == g)(functools.partial(finish_heads, g))
         each(n_seq, lambda o: send_out(h, o).start(), 1)
         back[h, me] = out[mine_rows, :]
         text_out[head_rows, :] = attended_t[:, img : img + txt]
-        for g in range(len(GROUPS)):
-            pl.when(h == g)(functools.partial(finish_heads, g))
         for g in range(len(GROUPS)):
             if g + 2 < len(GROUPS):
                 pl.when(h == g + 2)(functools.partial(add_second, g))

time: 117 us -> 117 us (level)
  no operation moved by 1% of the time
where the time goes in v2:
time: 117 us
  Pallas kernels  116 us (99%)
    pallas_call x1, Pallas kernels, on_device(): pl.pallas_call(functools.partial(kernel, (n_dp, n_seq, nx, ny)), out_shap...  113 us
    pallas_call x1, Pallas kernels, on_device(): pl.pallas_call(unpack_kernel, grid=(steps,), out_shape=(jax.ShapeDtypeStr...  3.73 us

profile of v2, /device:TPU:1, one launch (start us, length us, event | category | flops | bytes accessed | tf_op | source)
XLA Modules:
  0.0 117.0 jit_solution(15415604510363137357)
XLA Ops:
  0.6 112.6 %shard_map.129 = (bf16[5,8,128,256]{3,2,1,0:T(8,128)(2,1)}, bf16[320,333]{1,0:T(8,128)(2,1)}, f32[152,960]{1,0:T(8,128)}) custom-call(bf16[128,7680]{1,0:T(8,128)(2,1)} %bitcast.15, bf16[128,2560]{1,0:T(8,128)(2,1)} %bitcast.17, bf16[8,304,333]{2,1,0:T(8,128)(2,1)} %bitcast.16, bf16[304,333]{1,0:T(8,128)(2,1)} %bitcast.19, bf16[960,2432]{1,0:T(8,128)(2,1)} %bitcast.14, ...), custom_call_target="tpu_custom_call" | custom-call | tf_op jit(solution)/shard_map/pallas_call | solution.py:660
  113.2 3.7 %shard_map.130 = (bf16[128,2560]{1,0:T(8,128)(2,1)}, bf16[320,333]{1,0:T(8,128)(2,1)}, bf16[128,7680]{1,0:T(8,128)(2,1)}, f32[152,960]{1,0:T(8,128)}) custom-call(bf16[5,8,128,256]{3,2,1,0:T(8,128)(2,1)} %get-tuple-element.11.back, bf16[320,333]{1,0:T(8,128)(2,1)} %get-tuple-element.12.text_in, f32[152,960]{1,0:T(8,128)} %get-tuple-element.13.d_w_in), custom_call_target="tpu_custom_call" | custom-call | tf_op jit(solution)/shard_map/pallas_call | solution.py:686
